TPU v7x, 32 devices: a whole 2x2x4 slice. The times are simulated.
32 devices in a mesh: row: 4 (over y, core), col: 4 (over z), depth: 2 (over x).
Axes of the slice: x: 2, y: 2, z: 4, core: 2. Of those that a mesh axis runs over, the one named last changes fastest.
Arguments:
- tokens: bfloat16 [256, 4096], P(('col', 'depth'), 'row'), may hold values from -6 to 6
- out_grad: bfloat16 [256, 4096], P(('col', 'depth'), 'row'), may hold values from -2 to 2
- w_in: bfloat16 [4096, 14336], P('row', 'col'), may hold values from -0.09375 to 0.09375
- b_in: float32 [14336], P('col'), may hold values from -3 to 3
- w_out: bfloat16 [14336, 4096], P('col', 'row'), may hold values from -0.046875 to 0.046875
Outputs:
- block_out: bfloat16 [256, 4096], P(('col', 'depth'), 'row')
- tokens_grad: bfloat16 [256, 4096], P(('col', 'depth'), 'row')
- w_in_grad: bfloat16 [4096, 14336], P('row', ('col', 'depth'))
- w_out_grad: bfloat16 [14336, 4096], P(('col', 'depth'), 'row')
- b_in_grad: float32 [14336], P('col')
All inputs are finite; a program needn't handle non-finite values.
Results may differ from a plain program's by a relative error of at most 0.005.
Values may be sent and summed in bfloat16 or wider, within the bound.
A program may use at most 64 MiB of HBM per device.

v0:
```python
import functools

import jax
import jax.numpy as jnp
from jax import lax
from jax.experimental import pallas as pl
from jax.experimental.pallas import tpu as pltpu
from jax.sharding import PartitionSpec as P

root_coeff = 0.7978845608028654
cubic_coeff = 0.044715


def gelu_parts(pre_act):
    inner_arg = root_coeff * (pre_act + cubic_coeff * pre_act * pre_act * pre_act)
    tangent = jnp.tanh(inner_arg)
    gelu_value = 0.5 * pre_act * (1.0 + tangent)
    gelu_slope = 0.5 * (1.0 + tangent) + 0.5 * pre_act * (1.0 - tangent * tangent) * root_coeff * (
        1.0 + 3.0 * cubic_coeff * pre_act * pre_act
    )
    return (gelu_value, gelu_slope)


def right_transposed(left_side, right_side):
    return lax.dot_general(
        left_side, right_side, (((1,), (1,)), ((), ())), preferred_element_type=jnp.float32
    )


def left_transposed(left_side, right_side):
    return lax.dot_general(
        left_side, right_side, (((0,), (0,)), ((), ())), preferred_element_type=jnp.float32
    )


def depth_rows(gathered, col_count, depth_index, depth_count):
    tile_rows = gathered.shape[0] // (col_count * depth_count)
    shaped = gathered.reshape(col_count, depth_count, tile_rows, gathered.shape[1])
    picked = lax.dynamic_index_in_dim(shaped, depth_index, 1, keepdims=False)
    return picked.reshape(col_count * tile_rows, gathered.shape[1])


def local(tokens, out_grad, w_in, b_in, w_out):
    col_count = lax.axis_size("col")
    depth_count = lax.axis_size("depth")
    tile_rows = tokens.shape[0]
    part_cols = w_in.shape[1] // depth_count
    depth_index = lax.axis_index("depth")
    all_input, all_grad = (
        lax.all_gather(tokens, ("col", "depth"), axis=0, tiled=True),
        lax.all_gather(out_grad, ("col", "depth"), axis=0, tiled=True),
    )
    plane_input = depth_rows(all_input, col_count, depth_index, depth_count)
    plane_grad = depth_rows(all_grad, col_count, depth_index, depth_count)
    pre_sum = lax.psum_scatter(
        jnp.dot(plane_input, w_in, preferred_element_type=jnp.float32),
        "row",
        scatter_dimension=0,
        tiled=True,
    )
    pre_share = pre_sum + b_in
    gelu_value, gelu_slope = gelu_parts(pre_share)
    plane_act = lax.all_gather(gelu_value.astype(jnp.bfloat16), "row", axis=0, tiled=True)
    block_out = lax.psum_scatter(
        jnp.dot(plane_act, w_out, preferred_element_type=jnp.float32),
        "col",
        scatter_dimension=0,
        tiled=True,
    ).astype(jnp.bfloat16)
    grad_share = lax.psum_scatter(
        right_transposed(plane_grad, w_out), "row", scatter_dimension=0, tiled=True
    )
    pre_grad = grad_share * gelu_slope
    plane_hgrad = lax.all_gather(pre_grad.astype(jnp.bfloat16), "row", axis=0, tiled=True)
    b_in_grad = lax.psum(jnp.sum(pre_grad, axis=0), ("row", "depth"))
    tokens_grad = lax.psum_scatter(
        right_transposed(plane_hgrad, w_in), "col", scatter_dimension=0, tiled=True
    ).astype(jnp.bfloat16)
    act_parts = lax.all_to_all(
        plane_act.reshape(col_count, tile_rows, w_in.shape[1]),
        "depth",
        split_axis=2,
        concat_axis=1,
        tiled=True,
    )
    act_parts = act_parts.reshape(-1, part_cols)
    hgrad_parts = lax.all_to_all(
        plane_hgrad.reshape(col_count, tile_rows, w_in.shape[1]),
        "depth",
        split_axis=2,
        concat_axis=1,
        tiled=True,
    )
    hgrad_parts = hgrad_parts.reshape(-1, part_cols)
    w_in_grad = left_transposed(all_input, hgrad_parts)
    w_out_grad = left_transposed(act_parts, all_grad)
    return (
        block_out,
        tokens_grad,
        w_in_grad.astype(jnp.bfloat16),
        w_out_grad.astype(jnp.bfloat16),
        b_in_grad,
    )


MESH = pl.DeviceIdType.MESH
TILE = 256
BF16 = jnp.bfloat16
F32 = jnp.float32


def block_kernel(
    col_count,
    tokens_ref, grad_ref, w_in_ref, bias_ref, w_out_ref,
    *refs,
):
    away = col_count - 1
    out_ref, tgrad_ref, bgrad_ref, tok_out, og_out, act_out, hg_out = refs[:7]
    tgrad_away = refs[7:7 + away]
    (
    tok, og, w_in, w_out, bias, b_all, part, part16, core_in, chip16, y_in, act, hg, slope,
    x_out, x_in, z_sum, z_out, z_in, b_acc, b_core, b_own, b_x,
    local_sem, z_ssem, z_rsem, x_ssem, x_rsem, c_ssem, c_rsem, y_ssem, y_rsem,
    a_ssem, a_rsem, rx_ssem, rx_rsem, rz_ssem, rz_rsem, b_ssem, b_rsem, out_sem,
    ) = refs[7 + away:]
    row = lax.axis_index("row")
    col = lax.axis_index("col")
    depth = lax.axis_index("depth")
    core = lax.rem(row, 2)
    core_peer = {"row": row + 1 - 2 * core}
    y_peer = {"row": lax.rem(row + 2, 4)}
    x_peer = {"depth": 1 - depth}
    hidden = w_in.shape[1]
    feats = w_in.shape[0]
    half = part.shape[4]

    def z_peer(step):
        return {"col": lax.rem(col + step, col_count)}

    def remote(src, dst, ssem, rsem, peer):
        return pltpu.make_async_remote_copy(
            src_ref=src, dst_ref=dst, send_sem=ssem, recv_sem=rsem, device_id=peer, device_id_type=MESH
        )

    base = pl.multiple_of(depth * hidden, 128)
    locals_ = [
        pltpu.make_async_copy(tokens_ref, tok.at[0, 0], local_sem.at[0]),
        pltpu.make_async_copy(w_in_ref.at[:, pl.ds(base, hidden)], w_in, local_sem.at[1]),
        pltpu.make_async_copy(grad_ref, og.at[0, 0], local_sem.at[2]),
        pltpu.make_async_copy(w_out_ref.at[pl.ds(base, hidden), :], w_out, local_sem.at[3]),
        pltpu.make_async_copy(bias_ref, bias, local_sem.at[4]),
    ]
    for copy in locals_:
        copy.start()

    barrier = pltpu.get_barrier_semaphore()
    peers = [z_peer(step) for step in range(1, col_count)] + [x_peer, y_peer, core_peer]
    for peer in peers:
        pl.semaphore_signal(barrier, inc=1, device_id=peer, device_id_type=MESH)
    pl.semaphore_wait(barrier, len(peers))

    sends = []

    def start(copy):
        copy.start()
        sends.append(copy)
        return copy

    def gather_start(which, src, dst):
        start(remote(src, dst.at[1, 0], x_ssem.at[which, 0], x_rsem.at[which, 0], x_peer))
        for step in range(1, col_count):
            start(remote(src, dst.at[0, step], z_ssem.at[which, step], z_rsem.at[which, step], z_peer(step)))

    def gather_own(which, dst):
        for step in range(1, col_count):
            block = dst.at[0, step]
            remote(block, block, z_ssem.at[which, step], z_rsem.at[which, step], z_peer(step)).wait_recv()
            start(remote(block, dst.at[1, step], x_ssem.at[which, step], x_rsem.at[which, step], x_peer))

    def gather_other(which, dst):
        for step in range(col_count):
            block = dst.at[1, step]
            remote(block, block, x_ssem.at[which, step], x_rsem.at[which, step], x_peer).wait_recv()

    def tile_of(i):
        return pl.ds(pl.multiple_of(i * TILE, TILE), TILE)

    def rows_of(buf, group):
        chunk, first, count = group
        value = buf[chunk, first:first + count]
        return value.reshape(-1, value.shape[-1])

    def slots(buf, group, *before):
        chunk, first, count = group
        return buf.at[(*before, chunk, pl.ds(first, count))]

    def sem_of(group):
        return group[0], min(group[1], 1)

    def product(which, group, multiply):
        chunk, first, count = group

        @pl.loop(0, hidden // TILE)
        def _(i):
            at = tile_of(i)
            value = multiply(rows_of(og if which else tok, group), at)
            for n in range(2 * count):
                piece = value[n * half:(n + 1) * half]
                part[which, chunk, n % 2, first + n // 2, :, at] = piece
                part16[which, chunk, n % 2, first + n // 2, :, at] = piece.astype(BF16)

        start(remote(
            part16.at[which, chunk, 1 - core, pl.ds(first, count)], slots(core_in, group, which),
            c_ssem.at[(which, *sem_of(group))], c_rsem.at[(which, *sem_of(group))], core_peer,
        ))

    def chip_sum(which, group):
        chunk, first, count = group
        landed = slots(core_in, group, which)
        remote(
            landed, landed, c_ssem.at[(which, *sem_of(group))], c_rsem.at[(which, *sem_of(group))], core_peer
        ).wait_recv()

        @pl.loop(0, hidden // TILE)
        def _(i):
            at = tile_of(i)
            for s in range(first, first + count):
                total = part[which, chunk, core, s, :, at] + core_in[which, chunk, s, :, at].astype(F32)
                chip16[which, chunk, s, :, at] = total.astype(BF16)

        start(remote(
            slots(chip16, group, which), slots(y_in, group, which),
            y_ssem.at[(which, *sem_of(group))], y_rsem.at[(which, *sem_of(group))], y_peer,
        ))

    def y_wait(which, group):
        landed = slots(y_in, group, which)
        remote(
            landed, landed, y_ssem.at[(which, *sem_of(group))], y_rsem.at[(which, *sem_of(group))], y_peer
        ).wait_recv()

    def row_sum(which, chunk, s, at):
        return chip16[which, chunk, s, :, at].astype(F32) + y_in[which, chunk, s, :, at].astype(F32)

    def share(which, group, buf, whose):
        chunk, first, count = group
        piece = buf.at[chunk, pl.ds(first, count), whose]
        return remote(
            piece, piece, a_ssem.at[(which, *sem_of(group))], a_rsem.at[(which, *sem_of(group))], core_peer
        )

    def activate(group):
        chunk, first, count = group
        y_wait(0, group)

        @pl.loop(0, hidden // TILE)
        def _(i):
            at = tile_of(i)
            bias_here = b_all[:, pl.ds(pl.multiple_of(depth * hidden + i * TILE, 128), TILE)]
            for s in range(first, first + count):
                value, slope_here = gelu_parts(row_sum(0, chunk, s, at) + bias_here)
                act[chunk, s, core, :, at] = value.astype(BF16)
                slope[chunk, s, :, at] = slope_here

        start(share(0, group, act, core))

    def hidden_grad(group, fresh):
        chunk, first, count = group
        y_wait(1, group)

        @pl.loop(0, hidden // TILE)
        def _(i):
            at = tile_of(i)
            total = None if fresh else b_acc[:, at]
            for s in range(first, first + count):
                pre_grad = row_sum(1, chunk, s, at) * slope[chunk, s, :, at]
                hg[chunk, s, core, :, at] = pre_grad.astype(BF16)
                here = jnp.sum(pre_grad, axis=0, keepdims=True)
                total = here if total is None else total + here
            b_acc[:, at] = total

        start(share(1, group, hg, core))

    def project(which, chunk, buf, multiply):
        tile_rows = x_out.shape[2]

        @pl.loop(0, feats // TILE)
        def _(i):
            at = tile_of(i)
            value = multiply(rows_of(buf, (chunk, 0, col_count)), at)
            for c in range(col_count):
                piece = value[c * tile_rows:(c + 1) * tile_rows]
                if chunk == 1:
                    x_out[which, c, :, at] = piece.astype(BF16)
                else:
                    z_sum[which, c, :, at] = piece

        if chunk == 1:
            start(remote(x_out.at[which], x_in.at[which], rx_ssem.at[which], rx_rsem.at[which], x_peer))

    def plane_sum(which):
        landed = x_in.at[which]
        remote(landed, landed, rx_ssem.at[which], rx_rsem.at[which], x_peer).wait_recv()
        for c in range(col_count):
            total = z_sum[which, c] + x_in[which, c].astype(F32)
            z_sum[which, c] = total
            z_out[which, c] = total.astype(BF16)
        for step in range(1, col_count):
            start(remote(
                z_out.at[which, col_count - step], z_in.at[which, step - 1],
                rz_ssem.at[which, step - 1], rz_rsem.at[which, step - 1], z_peer(step),
            ))

    def final_sum(which, result):
        for step in range(1, col_count):
            landed = z_in.at[which, step - 1]
            remote(
                landed, landed, rz_ssem.at[which, step - 1], rz_rsem.at[which, step - 1], z_peer(step)
            ).wait_recv()
        total = z_sum[which, 0]
        for step in range(1, col_count):
            total = total + z_in[which, step - 1].astype(F32)
        result[...] = total.astype(BF16)

    def keep(which, src, dst):
        copy = pltpu.make_async_copy(src, dst, out_sem.at[which])
        copy.start()
        return copy

    def pre_tile(value, at):
        return jnp.dot(value, w_in[:, at], preferred_element_type=F32)

    def back_tile(value, at):
        return right_transposed(value, w_out[at, :])

    near, far = (0, 0, col_count), (1, 0, col_count)

    gather_start(0, tokens_ref, tok)
    locals_[4].wait()
    b_all[...] = bias[...].reshape(1, 2 * hidden)
    locals_[0].wait()
    locals_[1].wait()
    gather_own(0, tok)
    gather_start(1, grad_ref, og)
    product(0, near, pre_tile)
    gather_other(0, tok)
    chip_sum(0, near)
    product(0, far, pre_tile)
    kept = [keep(0, tok, tok_out)]
    chip_sum(0, far)
    locals_[2].wait()
    locals_[3].wait()
    gather_own(1, og)
    product(1, near, back_tile)
    gather_other(1, og)
    kept.append(keep(1, og, og_out))
    product(1, far, back_tile)
    activate(near)
    chip_sum(1, far)
    chip_sum(1, near)
    activate(far)
    share(0, near, act, 1 - core).wait_recv()

    def forward(value, at):
        return jnp.dot(value, w_out[:, at], preferred_element_type=F32)

    def backward(value, at):
        return right_transposed(value, w_in[at, :])

    share(0, far, act, 1 - core).wait_recv()
    kept.append(keep(2, act, act_out))
    project(0, 1, act, forward)
    project(0, 0, act, forward)
    hidden_grad(far, True)
    share(1, far, hg, 1 - core).wait_recv()
    project(1, 1, hg, backward)
    plane_sum(0)
    hidden_grad(near, False)
    start(remote(b_acc, b_core, b_ssem.at[0], b_rsem.at[0], core_peer))
    share(1, near, hg, 1 - core).wait_recv()
    kept.append(keep(3, hg, hg_out))
    project(1, 0, hg, backward)
    remote(b_core, b_core, b_ssem.at[0], b_rsem.at[0], core_peer).wait_recv()
    b_own[...] = b_acc[...] + b_core[...]
    start(remote(b_own, b_x, b_ssem.at[1], b_rsem.at[1], x_peer))
    final_sum(0, out_ref)
    landed = x_in.at[1]
    remote(landed, landed, rx_ssem.at[1], rx_rsem.at[1], x_peer).wait_recv()
    tgrad_ref[...] = z_sum[1, 0] + x_in[1, 0].astype(F32)
    for step in range(1, col_count):
        total = z_sum[1, col_count - step] + x_in[1, col_count - step].astype(F32)
        tgrad_away[step - 1][...] = total.astype(BF16)
    remote(b_x, b_x, b_ssem.at[1], b_rsem.at[1], x_peer).wait_recv()
    b_all[:, pl.ds(base, hidden)] = b_own[...]
    b_all[:, pl.ds(pl.multiple_of((1 - depth) * hidden, 128), hidden)] = b_x[...]
    bgrad_ref[...] = b_all[...].reshape(2 * hidden)
    for copy in kept:
        copy.wait()
    for copy in sends:
        copy.wait_send()


def weight_kernel(
    tok_ref, og_ref, act_ref, hg_ref, out_ref, w_in_grad_ref, w_out_grad_ref, out_again, tok_turned,
):
    @pl.when(pl.program_id(0) == 0)
    def _():
        tok_turned[...] = tok_ref[...].T
        out_again[...] = out_ref[...]

    w_in_grad_ref[...] = jnp.dot(tok_turned[...], hg_ref[...], preferred_element_type=F32).astype(BF16)
    w_out_grad_ref[...] = left_transposed(act_ref[...], og_ref[...]).astype(BF16)


def fused(col_count, tokens, out_grad, w_in, b_in, w_out):
    tile_rows, feats = tokens.shape
    hidden = w_in.shape[1] // 2
    plane = col_count * tile_rows
    half = tile_rows // 2
    rows = 2 * plane
    anywhere = pl.BlockSpec(memory_space=pltpu.HBM)
    vmem = pl.BlockSpec(memory_space=pltpu.VMEM)
    dma = pltpu.SemaphoreType.DMA
    outs = pl.pallas_call(
        functools.partial(block_kernel, col_count),
        out_shape=[
            jax.ShapeDtypeStruct((tile_rows, feats), BF16),
            jax.ShapeDtypeStruct((tile_rows, feats), F32),
            jax.ShapeDtypeStruct((2 * hidden,), F32),
            jax.ShapeDtypeStruct((2, col_count, tile_rows, feats), BF16),
            jax.ShapeDtypeStruct((2, col_count, tile_rows, feats), BF16),
            jax.ShapeDtypeStruct((2, col_count, 2, half, hidden), BF16),
            jax.ShapeDtypeStruct((2, col_count, 2, half, hidden), BF16),
        ] + [jax.ShapeDtypeStruct((tile_rows, feats), BF16)] * (col_count - 1),
        in_specs=[anywhere] * 5,
        out_specs=[vmem, vmem, vmem, anywhere, anywhere, anywhere, anywhere] + [vmem] * (col_count - 1),
        scratch_shapes=[
            pltpu.VMEM((2, col_count, tile_rows, feats), BF16),
            pltpu.VMEM((2, col_count, tile_rows, feats), BF16),
            pltpu.VMEM((feats, hidden), BF16),
            pltpu.VMEM((hidden, feats), BF16),
            pltpu.VMEM((2 * hidden,), F32),
            pltpu.VMEM((1, 2 * hidden), F32),
            pltpu.VMEM((2, 2, 2, col_count, half, hidden), F32),
            pltpu.VMEM((2, 2, 2, col_count, half, hidden), BF16),
            pltpu.VMEM((2, 2, col_count, half, hidden), BF16),
            pltpu.VMEM((2, 2, col_count, half, hidden), BF16),
            pltpu.VMEM((2, 2, col_count, half, hidden), BF16),
            pltpu.VMEM((2, col_count, 2, half, hidden), BF16),
            pltpu.VMEM((2, col_count, 2, half, hidden), BF16),
            pltpu.VMEM((2, col_count, half, hidden), F32),
            pltpu.VMEM((2, col_count, tile_rows, feats), BF16),
            pltpu.VMEM((2, col_count, tile_rows, feats), BF16),
            pltpu.VMEM((2, col_count, tile_rows, feats), F32),
            pltpu.VMEM((2, col_count, tile_rows, feats), BF16),
            pltpu.VMEM((2, col_count - 1, tile_rows, feats), BF16),
            pltpu.VMEM((1, hidden), F32),
            pltpu.VMEM((1, hidden), F32),
            pltpu.VMEM((1, hidden), F32),
            pltpu.VMEM((1, hidden), F32),
            dma((5,)),
            dma((2, col_count)),
            dma((2, col_count)),
            dma((2, col_count)),
            dma((2, col_count)),
            dma((2, 2, 2)),
            dma((2, 2, 2)),
            dma((2, 2, 2)),
            dma((2, 2, 2)),
            dma((2, 2, 2)),
            dma((2, 2, 2)),
            dma((2,)),
            dma((2,)),
            dma((2, col_count - 1)),
            dma((2, col_count - 1)),
            dma((2,)),
            dma((2,)),
            dma((4,)),
        ],
        compiler_params=pltpu.CompilerParams(
            collective_id=0, has_side_effects=True, vmem_limit_bytes=44 * 2**20
        ),
        cost_estimate=pl.CostEstimate(
            flops=8 * rows * feats * hidden, bytes_accessed=8 * feats * hidden, transcendentals=rows * hidden
        ),
    )(tokens, out_grad, w_in, b_in, w_out)
    block_out, tokens_part, bias_grad, tok, og, act, hg = outs[:7]
    arrived = []
    for step, piece in enumerate(outs[7:], 1):
        to_peer = [(c, (c + step) % col_count) for c in range(col_count)]
        arrived.append(lax.ppermute(piece, "col", to_peer))
    whole_block = lambda i: (0, 0)
    w_in_grad, w_out_grad, block_out = pl.pallas_call(
        weight_kernel,
        grid=(hidden // TILE,),
        out_shape=[
            jax.ShapeDtypeStruct((feats, hidden), BF16),
            jax.ShapeDtypeStruct((hidden, feats), BF16),
            jax.ShapeDtypeStruct((tile_rows, feats), BF16),
        ],
        in_specs=[
            pl.BlockSpec((rows, feats), whole_block),
            pl.BlockSpec((rows, feats), whole_block),
            pl.BlockSpec((rows, TILE), lambda i: (0, i)),
            pl.BlockSpec((rows, TILE), lambda i: (0, i)),
            pl.BlockSpec((tile_rows, feats), whole_block),
        ],
        out_specs=[
            pl.BlockSpec((feats, TILE), lambda i: (0, i)),
            pl.BlockSpec((TILE, feats), lambda i: (i, 0)),
            pl.BlockSpec((tile_rows, feats), whole_block),
        ],
        scratch_shapes=[pltpu.VMEM((feats, rows), BF16)],
        compiler_params=pltpu.CompilerParams(vmem_limit_bytes=32 * 2**20),
        cost_estimate=pl.CostEstimate(
            flops=4 * rows * feats * hidden, bytes_accessed=4 * feats * hidden, transcendentals=0
        ),
    )(
        tok.reshape(rows, feats), og.reshape(rows, feats), act.reshape(rows, hidden), hg.reshape(rows, hidden),
        block_out,
    )
    tokens_grad = tokens_part
    for piece in arrived:
        tokens_grad = tokens_grad + piece.astype(F32)
    tokens_grad = tokens_grad.astype(BF16)
    return block_out, tokens_grad, w_in_grad, w_out_grad, bias_grad


def by_shape(mesh):
    def run(tokens, out_grad, w_in, b_in, w_out):
        depth_count = mesh.shape["depth"]
        fits = (
            mesh.shape["row"] == 4
            and depth_count == 2
            and mesh.shape["col"] > 1
            and tokens.shape[0] % 32 == 0
            and tokens.shape[1] % TILE == 0
            and w_in.shape[1] % (depth_count * TILE) == 0
        )
        if fits:
            return fused(mesh.shape["col"], tokens, out_grad, w_in, b_in, w_out)
        return local(tokens, out_grad, w_in, b_in, w_out)

    return run


def solution(mesh):
    return jax.shard_map(
        by_shape(mesh),
        mesh=mesh,
        in_specs=(
            P(("col", "depth"), "row"),
            P(("col", "depth"), "row"),
            P("row", "col"),
            P("col"),
            P("col", "row"),
        ),
        out_specs=(
            P(("col", "depth"), "row"),
            P(("col", "depth"), "row"),
            P("row", ("col", "depth")),
            P(("col", "depth"), "row"),
            P("col"),
        ),
        check_vma=False,
    )
```

profile of v0, /device:TPU:0, one launch (start us, length us, event | category | flops | bytes accessed | tf_op | source)
XLA Modules:
  0.0 61.9 jit_solution(15001397377264885738)
XLA Ops:
  0.6 0.0 copy-start
  0.6 0.8 %copy-done = bf16[32,1024]{1,0:T(8,128)(2,1)S(1)} copy-done((bf16[32,1024]{1,0:T(8,128)(2,1)S(1)}, bf16[32,1024]{1,0:T(8,128)(2,1)}, u32[]{:S(2)}) %copy-start) | copy-done | bytes 65560
  1.5 0.0 copy-start.1
  1.5 0.8 %copy-done.1 = bf16[32,1024]{1,0:T(8,128)(2,1)S(1)} copy-done((bf16[32,1024]{1,0:T(8,128)(2,1)S(1)}, bf16[32,1024]{1,0:T(8,128)(2,1)}, u32[]{:S(2)}) %copy-start.1) | copy-done | bytes 65560
  2.3 0.0 copy-start.2
  2.3 0.7 %copy-done.2 = f32[3584]{0:T(1024)S(1)} copy-done((f32[3584]{0:T(1024)S(1)}, f32[3584]{0:T(1024)}, u32[]{:S(2)}) %copy-start.2) | copy-done | bytes 14360
  3.0 46.7 %shard_map.92 = (bf16[32,1024]{1,0:T(8,128)(2,1)S(1)}, f32[32,1024]{1,0:T(8,128)S(1)}, f32[3584]{0:T(1024)S(1)}, bf16[2,4,32,1024]{3,2,1,0:T(8,128)(2,1)S(1)}, b...) custom-call(bf16[32,1024]{1,0:T(8,128)(2,1)S(1)} %copy-done, ...), custom_call_target="tpu_custom_call" | custom-call | flops 3758096384 | bytes 14680064 | tf_op jit(solution)/shard_map/pallas_call | solution.py:424
  49.7 1.7 %collective-permute-start = (bf16[32,1024]{1,0:T(8,128)(2,1)S(1)}, bf16[32,1024]{1,0:T(8,128)(2,1)S(1)}, u32[]{:S(2)}, u32[]{:S(2)}) collective-permute-start(bf16[32,1024]{1,0:T(8,128)(2,1)S(1)} %get-tuple-element.25), channel_id=1, source_target_pairs={{0,2},{2,4},{4,6},{6,0},{1,3},{3,5},{5,7},{7,1},{8,10},{10,12},{12... | collective-permute-start | bytes 196616 | tf_op jit(solution)/shard_map/ppermute | solution.py:491
  51.4 2.2 %collective-permute-start.1 = (bf16[32,1024]{1,0:T(8,128)(2,1)S(1)}, bf16[32,1024]{1,0:T(8,128)(2,1)S(1)}, u32[]{:S(2)}, u32[]{:S(2)}) collective-permute-start(bf16[32,1024]{1,0:T(8,128)(2,1)S(1)} %get-tuple-element.26), channel_id=1, source_target_pairs={{0,4},{2,6},{4,0},{6,2},{1,5},{3,7},{5,1},{7,3},{8,12},{10,14},{12... | collective-permute-start | bytes 196616 | tf_op jit(solution)/shard_map/ppermute | solution.py:491
  53.7 1.0 %collective-permute-start.2 = (bf16[32,1024]{1,0:T(8,128)(2,1)S(1)}, bf16[32,1024]{1,0:T(8,128)(2,1)S(1)}, u32[]{:S(2)}, u32[]{:S(2)}) collective-permute-start(bf16[32,1024]{1,0:T(8,128)(2,1)S(1)} %get-tuple-element.27), channel_id=1, source_target_pairs={{0,6},{2,0},{4,2},{6,4},{1,7},{3,1},{5,3},{7,5},{8,14},{10,8},{12,... | collective-permute-start | bytes 196616 | tf_op jit(solution)/shard_map/ppermute | solution.py:491
  54.7 5.9 %shard_map.93 = (bf16[1024,1792]{1,0:T(8,128)(2,1)}, bf16[1792,1024]{1,0:T(8,128)(2,1)}, bf16[32,1024]{1,0:T(8,128)(2,1)}) custom-call(bf16[256,1024]{1,0:T(8,128)(2,1)S(1)} %bitcast.6, bf16[256,1024]{1,0:T(8,128)(2,1)S(1)} %bitcast.7, bf16[256,1792]{1,0:T(8,128)(2,1)S(1)} %bitcast.4, bf16[256,1792]{1,0:T(8,128)(2,1)S(1)} %bitcast.5, ...), custom_call_target="tpu_custom_call" | custom-call | flops 1879048192 | bytes 7340032 | tf_op jit(solution)/shard_map/pallas_call | solution.py:493
  60.6 0.0 collective-permute-done
  60.6 0.0 collective-permute-done.1
  60.6 0.0 collective-permute-done.2
  60.6 0.7 %add_convert_fusion = bf16[32,1024]{1,0:T(8,128)(2,1)} fusion(bf16[32,1024]{1,0:T(8,128)(2,1)S(1)} %collective-permute-done.2, bf16[32,1024]{1,0:T(8,128)(2,1)S(1)} %collective-permute-done.1, f32[32,1024]{1,0:T(8,128)S(1)} %get-tuple-element.24, bf16[32,1024]{1,0:T(8,128)(2,1)S(1)} %collective-permute-done), kind=kLoop, calls=%fused_computation | loop fusion | flops 229376 | bytes 393216 | tf_op jit(solution)/shard_map/convert_element_type | solution.py:525
  61.3 0.6 copy.11
Async XLA Ops:
  0.6 0.8 %copy-start = (bf16[32,1024]{1,0:T(8,128)(2,1)S(1)}, bf16[32,1024]{1,0:T(8,128)(2,1)}, u32[]{:S(2)}) copy-start(bf16[32,1024]{1,0:T(8,128)(2,1)} %tokens_ref.1) | copy-start | bytes 196612
  1.5 0.8 %copy-start.1 = (bf16[32,1024]{1,0:T(8,128)(2,1)S(1)}, bf16[32,1024]{1,0:T(8,128)(2,1)}, u32[]{:S(2)}) copy-start(bf16[32,1024]{1,0:T(8,128)(2,1)} %grad_ref.1) | copy-start | bytes 196612
  2.3 0.7 %copy-start.2 = (f32[3584]{0:T(1024)S(1)}, f32[3584]{0:T(1024)}, u32[]{:S(2)}) copy-start(f32[3584]{0:T(1024)} %bias_ref.1) | copy-start | bytes 43012
  49.7 10.8 %collective-permute-start = (bf16[32,1024]{1,0:T(8,128)(2,1)S(1)}, bf16[32,1024]{1,0:T(8,128)(2,1)S(1)}, u32[]{:S(2)}, u32[]{:S(2)}) collective-permute-start(bf16[32,1024]{1,0:T(8,128)(2,1)S(1)} %get-tuple-element.25), channel_id=1, source_target_pairs={{0,2},{2,4},{4,6},{6,0},{1,3},{3,5},{5,7},{7,1},{8,10},{10,12},{12... | collective-permute-start | bytes 196616 | tf_op jit(solution)/shard_map/ppermute | solution.py:491
  51.4 9.2 %collective-permute-start.1 = (bf16[32,1024]{1,0:T(8,128)(2,1)S(1)}, bf16[32,1024]{1,0:T(8,128)(2,1)S(1)}, u32[]{:S(2)}, u32[]{:S(2)}) collective-permute-start(bf16[32,1024]{1,0:T(8,128)(2,1)S(1)} %get-tuple-element.26), channel_id=1, source_target_pairs={{0,4},{2,6},{4,0},{6,2},{1,5},{3,7},{5,1},{7,3},{8,12},{10,14},{12... | collective-permute-start | bytes 196616 | tf_op jit(solution)/shard_map/ppermute | solution.py:491
  53.7 6.9 %collective-permute-start.2 = (bf16[32,1024]{1,0:T(8,128)(2,1)S(1)}, bf16[32,1024]{1,0:T(8,128)(2,1)S(1)}, u32[]{:S(2)}, u32[]{:S(2)}) collective-permute-start(bf16[32,1024]{1,0:T(8,128)(2,1)S(1)} %get-tuple-element.27), channel_id=1, source_target_pairs={{0,6},{2,0},{4,2},{6,4},{1,7},{3,1},{5,3},{7,5},{8,14},{10,8},{12,... | collective-permute-start | bytes 196616 | tf_op jit(solution)/shard_map/ppermute | solution.py:491
where the time goes:
time: 62.1 us; the launch traced here: 61.9 us
  Pallas kernels  52.6 us (85%)
  starting transfers between devices  4.94 us (8%)
  local copies, waits for them, and re-layouts  2.99 us (5%)
  between operations  0.67 us (1%)
  other arithmetic  0.66 us (1%)
    pallas_call x1, Pallas kernels, fused(): pl.pallas_call(functools.partial(block_kernel, col_count), out_shape=[jax...  46.7 us
    pallas_call x1, Pallas kernels, fused(): pl.pallas_call(weight_kernel, grid=(hidden // TILE,), out_shape=[jax.Shap...  5.89 us
    ppermute x3, starting transfers between devices, fused(): arrived.append(lax.ppermute(piece, 'col', to_peer))  4.94 us
    unnamed x7, local copies, waits for them, and re-layouts  2.99 us
  transfers between devices with their start and end apart: 3, of which 0 were waited for; matrix products, arithmetic and copies ran while one was open for 0% of the time, Pallas kernels for 10%

commit v1 on v0

--- a/solution.py
+++ b/solution.py
@@ -166,8 +166,10 @@
         sends.append(copy)
         return copy
 
-    def gather_start(which, src, dst):
+    def pair_start(which, src, dst):
         start(remote(src, dst.at[1, 0], x_ssem.at[which, 0], x_rsem.at[which, 0], x_peer))
+
+    def line_start(which, src, dst):
         for step in range(1, col_count):
             start(remote(src, dst.at[0, step], z_ssem.at[which, step], z_rsem.at[which, step], z_peer(step)))
 
@@ -177,87 +179,78 @@
             remote(block, block, z_ssem.at[which, step], z_rsem.at[which, step], z_peer(step)).wait_recv()
             start(remote(block, dst.at[1, step], x_ssem.at[which, step], x_rsem.at[which, step], x_peer))
 
+    def other_wait(which, dst, step):
+        block = dst.at[1, step]
+        remote(block, block, x_ssem.at[which, step], x_rsem.at[which, step], x_peer).wait_recv()
+
     def gather_other(which, dst):
-        for step in range(col_count):
-            block = dst.at[1, step]
-            remote(block, block, x_ssem.at[which, step], x_rsem.at[which, step], x_peer).wait_recv()
+        for step in range(1, col_count):
+            other_wait(which, dst, step)
 
     def tile_of(i):
         return pl.ds(pl.multiple_of(i * TILE, TILE), TILE)
 
+    def cut(group):
+        return pl.ds(group[1][0], len(group[1])), pl.ds(group[2][0], len(group[2]))
+
     def rows_of(buf, group):
-        chunk, first, count = group
-        value = buf[chunk, first:first + count]
+        value = buf[(*cut(group),)]
         return value.reshape(-1, value.shape[-1])
 
-    def slots(buf, group, *before):
-        chunk, first, count = group
-        return buf.at[(*before, chunk, pl.ds(first, count))]
-
-    def sem_of(group):
-        return group[0], min(group[1], 1)
+    def places(group):
+        return [(chunk, s) for chunk in group[1] for s in group[2]]
 
     def product(which, group, multiply):
-        chunk, first, count = group
-
         @pl.loop(0, hidden // TILE)
         def _(i):
             at = tile_of(i)
             value = multiply(rows_of(og if which else tok, group), at)
-            for n in range(2 * count):
-                piece = value[n * half:(n + 1) * half]
-                part[which, chunk, n % 2, first + n // 2, :, at] = piece
-                part16[which, chunk, n % 2, first + n // 2, :, at] = piece.astype(BF16)
+            for n, (chunk, s) in enumerate(places(group)):
+                for k in range(2):
+                    piece = value[(2 * n + k) * half:(2 * n + k + 1) * half]
+                    part[which, k, chunk, s, :, at] = piece
+                    part16[which, k, chunk, s, :, at] = piece.astype(BF16)
 
         start(remote(
-            part16.at[which, chunk, 1 - core, pl.ds(first, count)], slots(core_in, group, which),
-            c_ssem.at[(which, *sem_of(group))], c_rsem.at[(which, *sem_of(group))], core_peer,
+            part16.at[(which, 1 - core, *cut(group))], core_in.at[(which, *cut(group))],
+            c_ssem.at[which, group[0]], c_rsem.at[which, group[0]], core_peer,
         ))
 
     def chip_sum(which, group):
-        chunk, first, count = group
-        landed = slots(core_in, group, which)
-        remote(
-            landed, landed, c_ssem.at[(which, *sem_of(group))], c_rsem.at[(which, *sem_of(group))], core_peer
-        ).wait_recv()
+        landed = core_in.at[(which, *cut(group))]
+        remote(landed, landed, c_ssem.at[which, group[0]], c_rsem.at[which, group[0]], core_peer).wait_recv()
 
         @pl.loop(0, hidden // TILE)
         def _(i):
             at = tile_of(i)
-            for s in range(first, first + count):
-                total = part[which, chunk, core, s, :, at] + core_in[which, chunk, s, :, at].astype(F32)
+            for chunk, s in places(group):
+                total = part[which, core, chunk, s, :, at] + core_in[which, chunk, s, :, at].astype(F32)
                 chip16[which, chunk, s, :, at] = total.astype(BF16)
 
         start(remote(
-            slots(chip16, group, which), slots(y_in, group, which),
-            y_ssem.at[(which, *sem_of(group))], y_rsem.at[(which, *sem_of(group))], y_peer,
+            chip16.at[(which, *cut(group))], y_in.at[(which, *cut(group))],
+            y_ssem.at[which, group[0]], y_rsem.at[which, group[0]], y_peer,
         ))
 
     def y_wait(which, group):
-        landed = slots(y_in, group, which)
-        remote(
-            landed, landed, y_ssem.at[(which, *sem_of(group))], y_rsem.at[(which, *sem_of(group))], y_peer
-        ).wait_recv()
+        landed = y_in.at[(which, *cut(group))]
+        remote(landed, landed, y_ssem.at[which, group[0]], y_rsem.at[which, group[0]], y_peer).wait_recv()
 
     def row_sum(which, chunk, s, at):
         return chip16[which, chunk, s, :, at].astype(F32) + y_in[which, chunk, s, :, at].astype(F32)
 
     def share(which, group, buf, whose):
-        chunk, first, count = group
-        piece = buf.at[chunk, pl.ds(first, count), whose]
-        return remote(
-            piece, piece, a_ssem.at[(which, *sem_of(group))], a_rsem.at[(which, *sem_of(group))], core_peer
-        )
+        piece = buf.at[(*cut(group), whose)]
+        return remote(piece, piece, a_ssem.at[which, group[0]], a_rsem.at[which, group[0]], core_peer)
 
     def activate(group):
-        chunk, first, count = group
         y_wait(0, group)
 
         @pl.loop(0, hidden // TILE)
         def _(i):
             at = tile_of(i)
             bias_here = b_all[:, pl.ds(pl.multiple_of(depth * hidden + i * TILE, 128), TILE)]
-            for s in range(first, first + count):
+            for chunk, s in places(group):
                 value, slope_here = gelu_parts(row_sum(0, chunk, s, at) + bias_here)
                 act[chunk, s, core, :, at] = value.astype(BF16)
                 slope[chunk, s, :, at] = slope_here
@@ -265,14 +258,13 @@
         start(share(0, group, act, core))
 
     def hidden_grad(group, fresh):
-        chunk, first, count = group
         y_wait(1, group)
 
         @pl.loop(0, hidden // TILE)
         def _(i):
             at = tile_of(i)
             total = None if fresh else b_acc[:, at]
-            for s in range(first, first + count):
+            for chunk, s in places(group):
                 pre_grad = row_sum(1, chunk, s, at) * slope[chunk, s, :, at]
                 hg[chunk, s, core, :, at] = pre_grad.astype(BF16)
                 here = jnp.sum(pre_grad, axis=0, keepdims=True)
@@ -287,7 +279,7 @@
         @pl.loop(0, feats // TILE)
         def _(i):
             at = tile_of(i)
-            value = multiply(rows_of(buf, (chunk, 0, col_count)), at)
+            value = multiply(rows_of(buf, (0, (chunk,), range(col_count))), at)
             for c in range(col_count):
                 piece = value[c * tile_rows:(c + 1) * tile_rows]
                 if chunk == 1:
@@ -333,33 +325,43 @@
     def back_tile(value, at):
         return right_transposed(value, w_out[at, :])
 
-    near, far = (0, 0, col_count), (1, 0, col_count)
-
-    gather_start(0, tokens_ref, tok)
+    steps = range(1, col_count)
+    pair, far, near = (0, (0, 1), (0,)), (1, (1,), steps), (2, (0,), steps)
+
+    pair_start(0, tokens_ref, tok)
+    line_start(0, tokens_ref, tok)
+    pair_start(1, grad_ref, og)
     locals_[4].wait()
     b_all[...] = bias[...].reshape(1, 2 * hidden)
     locals_[0].wait()
     locals_[1].wait()
+    other_wait(0, tok, 0)
+    product(0, pair, pre_tile)
+    locals_[2].wait()
+    locals_[3].wait()
+    other_wait(1, og, 0)
+    product(1, pair, back_tile)
+    chip_sum(0, pair)
+    chip_sum(1, pair)
     gather_own(0, tok)
-    gather_start(1, grad_ref, og)
+    line_start(1, grad_ref, og)
     product(0, near, pre_tile)
     gather_other(0, tok)
-    chip_sum(0, near)
     product(0, far, pre_tile)
     kept = [keep(0, tok, tok_out)]
     chip_sum(0, far)
-    locals_[2].wait()
-    locals_[3].wait()
+    chip_sum(0, near)
     gather_own(1, og)
     product(1, near, back_tile)
+    activate(pair)
     gather_other(1, og)
     kept.append(keep(1, og, og_out))
     product(1, far, back_tile)
-    activate(near)
+    activate(far)
     chip_sum(1, far)
     chip_sum(1, near)
-    activate(far)
-    share(0, near, act, 1 - core).wait_recv()
+    share(0, pair, act, 1 - core).wait_recv()
+    share(0, far, act, 1 - core).wait_recv()
 
     def forward(value, at):
         return jnp.dot(value, w_out[:, at], preferred_element_type=F32)
@@ -367,11 +369,14 @@
     def backward(value, at):
         return right_transposed(value, w_in[at, :])
 
-    share(0, far, act, 1 - core).wait_recv()
+    project(0, 1, act, forward)
+    activate(near)
+    hidden_grad(pair, True)
+    share(0, near, act, 1 - core).wait_recv()
     kept.append(keep(2, act, act_out))
-    project(0, 1, act, forward)
     project(0, 0, act, forward)
-    hidden_grad(far, True)
+    hidden_grad(far, False)
+    share(1, pair, hg, 1 - core).wait_recv()
     share(1, far, hg, 1 - core).wait_recv()
     project(1, 1, hg, backward)
     plane_sum(0)
@@ -379,10 +384,10 @@
     start(remote(b_acc, b_core, b_ssem.at[0], b_rsem.at[0], core_peer))
     share(1, near, hg, 1 - core).wait_recv()
     kept.append(keep(3, hg, hg_out))
-    project(1, 0, hg, backward)
     remote(b_core, b_core, b_ssem.at[0], b_rsem.at[0], core_peer).wait_recv()
     b_own[...] = b_acc[...] + b_core[...]
     start(remote(b_own, b_x, b_ssem.at[1], b_rsem.at[1], x_peer))
+    project(1, 0, hg, backward)
     final_sum(0, out_ref)
     landed = x_in.at[1]
     remote(landed, landed, rx_ssem.at[1], rx_rsem.at[1], x_peer).wait_recv()
@@ -463,12 +468,12 @@
             dma((2, col_count)),
             dma((2, col_count)),
             dma((2, col_count)),
-            dma((2, 2, 2)),
-            dma((2, 2, 2)),
-            dma((2, 2, 2)),
-            dma((2, 2, 2)),
-            dma((2, 2, 2)),
-            dma((2, 2, 2)),
+            dma((2, 3)),
+            dma((2, 3)),
+            dma((2, 3)),
+            dma((2, 3)),
+            dma((2, 3)),
+            dma((2, 3)),
             dma((2,)),
             dma((2,)),
             dma((2, col_count - 1)),

time: 62.1 us -> 63.5 us (1.023)
  Pallas kernels: 52.6 us -> 55.1 us
  starting transfers between devices: 4.94 us -> 3.88 us
    pallas_call x1, Pallas kernels: 46.7 us -> 49.2 us  [fused(): pl.pallas_call(functools.partial(block_kernel, col_count), out_shape=[jax...]
    ppermute x3, starting transfers between devices: 4.94 us -> 3.88 us  [fused(): arrived.append(lax.ppermute(piece, 'col', to_peer))]
  transfers between devices with their start and end apart: 3 -> 3, of which waited for: 0 -> 0; matrix products, arithmetic and copies ran while one was open for 0% -> 0% of each run, Pallas kernels for 10% -> 9%
where the time goes in v1:
time: 63.5 us; the launch traced here: 63.3 us
  Pallas kernels  55.1 us (87%)
  starting transfers between devices  3.88 us (6%)
  local copies, waits for them, and re-layouts  2.99 us (5%)
  between operations  0.67 us (1%)
  other arithmetic  0.66 us (1%)
    pallas_call x1, Pallas kernels, fused(): pl.pallas_call(functools.partial(block_kernel, col_count), out_shape=[jax...  49.2 us
    pallas_call x1, Pallas kernels, fused(): pl.pallas_call(weight_kernel, grid=(hidden // TILE,), out_shape=[jax.Shap...  5.89 us
    ppermute x3, starting transfers between devices, fused(): arrived.append(lax.ppermute(piece, 'col', to_peer))  3.88 us
    unnamed x7, local copies, waits for them, and re-layouts  2.99 us
  transfers between devices with their start and end apart: 3, of which 0 were waited for; matrix products, arithmetic and copies ran while one was open for 0% of the time, Pallas kernels for 9%

profile of v1, /device:TPU:0, one launch (start us, length us, event | category | flops | bytes accessed | tf_op | source)
XLA Modules:
  0.0 63.3 jit_solution(7994953486124925356)
XLA Ops:
  0.6 0.0 copy-start
  0.6 0.8 %copy-done = bf16[32,1024]{1,0:T(8,128)(2,1)S(1)} copy-done((bf16[32,1024]{1,0:T(8,128)(2,1)S(1)}, bf16[32,1024]{1,0:T(8,128)(2,1)}, u32[]{:S(2)}) %copy-start) | copy-done | bytes 65560
  1.5 0.0 copy-start.1
  1.5 0.8 %copy-done.1 = bf16[32,1024]{1,0:T(8,128)(2,1)S(1)} copy-done((bf16[32,1024]{1,0:T(8,128)(2,1)S(1)}, bf16[32,1024]{1,0:T(8,128)(2,1)}, u32[]{:S(2)}) %copy-start.1) | copy-done | bytes 65560
  2.3 0.0 copy-start.2
  2.3 0.7 %copy-done.2 = f32[3584]{0:T(1024)S(1)} copy-done((f32[3584]{0:T(1024)S(1)}, f32[3584]{0:T(1024)}, u32[]{:S(2)}) %copy-start.2) | copy-done | bytes 14360
  3.0 49.2 %shard_map.92 = (bf16[32,1024]{1,0:T(8,128)(2,1)S(1)}, f32[32,1024]{1,0:T(8,128)S(1)}, f32[3584]{0:T(1024)S(1)}, bf16[2,4,32,1024]{3,2,1,0:T(8,128)(2,1)S(1)}, b...) custom-call(bf16[32,1024]{1,0:T(8,128)(2,1)S(1)} %copy-done, ...), custom_call_target="tpu_custom_call" | custom-call | flops 3758096384 | bytes 14680064 | tf_op jit(solution)/shard_map/pallas_call | solution.py:429
  52.2 0.3 collective-permute-start
  52.5 2.4 %collective-permute-start.1 = (bf16[32,1024]{1,0:T(8,128)(2,1)S(1)}, bf16[32,1024]{1,0:T(8,128)(2,1)S(1)}, u32[]{:S(2)}, u32[]{:S(2)}) collective-permute-start(bf16[32,1024]{1,0:T(8,128)(2,1)S(1)} %get-tuple-element.26), channel_id=1, source_target_pairs={{0,4},{2,6},{4,0},{6,2},{1,5},{3,7},{5,1},{7,3},{8,12},{10,14},{12... | collective-permute-start | bytes 196616 | tf_op jit(solution)/shard_map/ppermute | solution.py:496
  54.8 1.3 %collective-permute-start.2 = (bf16[32,1024]{1,0:T(8,128)(2,1)S(1)}, bf16[32,1024]{1,0:T(8,128)(2,1)S(1)}, u32[]{:S(2)}, u32[]{:S(2)}) collective-permute-start(bf16[32,1024]{1,0:T(8,128)(2,1)S(1)} %get-tuple-element.27), channel_id=1, source_target_pairs={{0,6},{2,0},{4,2},{6,4},{1,7},{3,1},{5,3},{7,5},{8,14},{10,8},{12,... | collective-permute-start | bytes 196616 | tf_op jit(solution)/shard_map/ppermute | solution.py:496
  56.1 5.9 %shard_map.93 = (bf16[1024,1792]{1,0:T(8,128)(2,1)}, bf16[1792,1024]{1,0:T(8,128)(2,1)}, bf16[32,1024]{1,0:T(8,128)(2,1)}) custom-call(bf16[256,1024]{1,0:T(8,128)(2,1)S(1)} %bitcast.6, bf16[256,1024]{1,0:T(8,128)(2,1)S(1)} %bitcast.7, bf16[256,1792]{1,0:T(8,128)(2,1)S(1)} %bitcast.4, bf16[256,1792]{1,0:T(8,128)(2,1)S(1)} %bitcast.5, ...), custom_call_target="tpu_custom_call" | custom-call | flops 1879048192 | bytes 7340032 | tf_op jit(solution)/shard_map/pallas_call | solution.py:498
  62.0 0.0 collective-permute-done
  62.0 0.0 collective-permute-done.1
  62.0 0.0 collective-permute-done.2
  62.0 0.7 %add_convert_fusion = bf16[32,1024]{1,0:T(8,128)(2,1)} fusion(bf16[32,1024]{1,0:T(8,128)(2,1)S(1)} %collective-permute-done.2, bf16[32,1024]{1,0:T(8,128)(2,1)S(1)} %collective-permute-done.1, f32[32,1024]{1,0:T(8,128)S(1)} %get-tuple-element.24, bf16[32,1024]{1,0:T(8,128)(2,1)S(1)} %collective-permute-done), kind=kLoop, calls=%fused_computation | loop fusion | flops 229376 | bytes 393216 | tf_op jit(solution)/shard_map/convert_element_type | solution.py:530
  62.7 0.6 copy.11
Async XLA Ops:
  0.6 0.8 %copy-start = (bf16[32,1024]{1,0:T(8,128)(2,1)S(1)}, bf16[32,1024]{1,0:T(8,128)(2,1)}, u32[]{:S(2)}) copy-start(bf16[32,1024]{1,0:T(8,128)(2,1)} %tokens_ref.1) | copy-start | bytes 196612
  1.5 0.8 %copy-start.1 = (bf16[32,1024]{1,0:T(8,128)(2,1)S(1)}, bf16[32,1024]{1,0:T(8,128)(2,1)}, u32[]{:S(2)}) copy-start(bf16[32,1024]{1,0:T(8,128)(2,1)} %grad_ref.1) | copy-start | bytes 196612
  2.3 0.7 %copy-start.2 = (f32[3584]{0:T(1024)S(1)}, f32[3584]{0:T(1024)}, u32[]{:S(2)}) copy-start(f32[3584]{0:T(1024)} %bias_ref.1) | copy-start | bytes 43012
  52.2 9.8 %collective-permute-start = (bf16[32,1024]{1,0:T(8,128)(2,1)S(1)}, bf16[32,1024]{1,0:T(8,128)(2,1)S(1)}, u32[]{:S(2)}, u32[]{:S(2)}) collective-permute-start(bf16[32,1024]{1,0:T(8,128)(2,1)S(1)} %get-tuple-element.25), channel_id=1, source_target_pairs={{0,2},{2,4},{4,6},{6,0},{1,3},{3,5},{5,7},{7,1},{8,10},{10,12},{12... | collective-permute-start | bytes 196616 | tf_op jit(solution)/shard_map/ppermute | solution.py:496
  52.5 9.5 %collective-permute-start.1 = (bf16[32,1024]{1,0:T(8,128)(2,1)S(1)}, bf16[32,1024]{1,0:T(8,128)(2,1)S(1)}, u32[]{:S(2)}, u32[]{:S(2)}) collective-permute-start(bf16[32,1024]{1,0:T(8,128)(2,1)S(1)} %get-tuple-element.26), channel_id=1, source_target_pairs={{0,4},{2,6},{4,0},{6,2},{1,5},{3,7},{5,1},{7,3},{8,12},{10,14},{12... | collective-permute-start | bytes 196616 | tf_op jit(solution)/shard_map/ppermute | solution.py:496
  54.8 7.2 %collective-permute-start.2 = (bf16[32,1024]{1,0:T(8,128)(2,1)S(1)}, bf16[32,1024]{1,0:T(8,128)(2,1)S(1)}, u32[]{:S(2)}, u32[]{:S(2)}) collective-permute-start(bf16[32,1024]{1,0:T(8,128)(2,1)S(1)} %get-tuple-element.27), channel_id=1, source_target_pairs={{0,6},{2,0},{4,2},{6,4},{1,7},{3,1},{5,3},{7,5},{8,14},{10,8},{12,... | collective-permute-start | bytes 196616 | tf_op jit(solution)/shard_map/ppermute | solution.py:496
